TPU v7x, 32 devices: a whole 2x2x4 slice. The times are simulated.
32 devices in a mesh: lon: 4 (over z), lev: 2 (over x), lat: 4 (over y, core).
Axes of the slice: x: 2, y: 2, z: 4, core: 2. Of those that a mesh axis runs over, the one named last changes fastest.
Arguments:
- features: bfloat16 [32, 128, 8, 192], P('lat', 'lon', 'lev'), may hold values from -6 to 6
- conv_weight: bfloat16 [8, 3, 3, 192, 192], P('lev'), may hold values from -0.15625 to 0.15625
- join_weight: bfloat16 [8, 192, 8, 192], replicated, may hold values from -0.15625 to 0.15625
- joined_grad: bfloat16 [32, 128, 8, 192], P('lat', 'lon', 'lev'), may hold values from -6 to 6
Outputs:
- joined_fields: float32 [32, 128, 8, 192], P('lat', 'lon', 'lev')
- input_grad: float32 [32, 128, 8, 192], P('lat', 'lon', 'lev')
- conv_grad: float32 [8, 3, 3, 192, 192], P('lev', None, None, 'lon')
- join_grad: float32 [8, 192, 8, 192], P(None, 'lon', 'lev')
All inputs are finite; a program needn't handle non-finite values.
Results may differ from a plain program's by a relative error of at most 0.0029.
Values may be sent and summed in bfloat16 or wider, within the bound.
A program may use at most 128 MiB of HBM per device.

v0:
```python
from functools import partial
import math

import jax
import jax.numpy as jnp
from jax import lax
from jax.sharding import PartitionSpec as P


def extended(x, sides, width, wrap):
    for axis, dim in sides:
        count, length = (lax.axis_size(axis), x.shape[dim])
        up = [(i, (i + 1) % count) for i in range(count if wrap else count - 1)]
        down = [(j, i) for i, j in up]
        last = lax.slice_in_dim(x, length - width, length, axis=dim)
        first = lax.slice_in_dim(x, 0, width, axis=dim)
        before = lax.ppermute(last, axis, up)
        after = lax.ppermute(first, axis, down)
        x = jnp.concatenate([before, x, after], axis=dim)
    return x


def extend(grid_field):
    lon_wide = extended(grid_field, (("lon", 1),), 1, True)
    return extended(lon_wide, (("lat", 0),), 1, False)


def forward_taps(padded, weight):
    row_count = padded.shape[0] - 2
    col_count = padded.shape[1] - 2
    summed = None
    for tap_row in range(3):
        for tap_col in range(3):
            window = padded[tap_row : tap_row + row_count, tap_col : tap_col + col_count]
            product_term = jnp.einsum(
                "abli,lio->ablo",
                window,
                weight[:, tap_row, tap_col],
                preferred_element_type=jnp.float32,
            )
            summed = product_term if summed is None else summed + product_term
    return summed


def backward_taps(padded, weight):
    row_count = padded.shape[0] - 2
    col_count = padded.shape[1] - 2
    summed = None
    for tap_row in range(3):
        for tap_col in range(3):
            window = padded[
                2 - tap_row : 2 - tap_row + row_count, 2 - tap_col : 2 - tap_col + col_count
            ]
            product_term = jnp.einsum(
                "ablo,lio->abli",
                window,
                weight[:, tap_row, tap_col],
                preferred_element_type=jnp.float32,
            )
            summed = product_term if summed is None else summed + product_term
    return summed


def weight_taps(padded, pre_grad):
    row_count = pre_grad.shape[0]
    col_count = pre_grad.shape[1]
    rows_list = []
    for tap_row in range(3):
        tap_list = []
        for tap_col in range(3):
            window = padded[tap_row : tap_row + row_count, tap_col : tap_col + col_count]
            tap_list.append(
                jnp.einsum("abli,ablo->lio", window, pre_grad, preferred_element_type=jnp.float32)
            )
        rows_list.append(jnp.stack(tap_list, axis=1))
    return jnp.stack(rows_list, axis=1)


def per_device(features, conv_weight, join_weight, joined_grad):
    lat_rows, lon_cols, lev_local, channels = features.shape
    lev_total = join_weight.shape[0]
    cell_count = lat_rows * lon_cols
    grid_scale = 1.0 / math.sqrt(lat_rows * lax.axis_size("lat") * lon_cols * lax.axis_size("lon"))
    padded_input = extend(features)
    pre_act = forward_taps(padded_input, conv_weight)
    gelu_out, pull_back = jax.vjp(partial(jax.nn.gelu, approximate=True), pre_act)
    activation = gelu_out.astype(jnp.bfloat16)
    all_levels = lax.all_gather(activation, "lev", axis=2, tiled=True)
    flat_all = all_levels.reshape(cell_count, lev_total * channels)
    level_start = lax.axis_index("lev") * lev_local
    own_columns = lax.dynamic_slice_in_dim(join_weight, level_start, lev_local, 2).reshape(
        lev_total * channels, lev_local * channels
    )
    joined_fields = jnp.dot(flat_all, own_columns, preferred_element_type=jnp.float32).reshape(
        features.shape
    )
    flat_grad = joined_grad.reshape(cell_count, lev_local * channels)
    partial_terms = lax.dot_general(
        flat_grad, own_columns, (((1,), (1,)), ((), ())), preferred_element_type=jnp.float32
    )
    act_grad = lax.psum_scatter(
        partial_terms.reshape(lat_rows, lon_cols, lev_total, channels),
        "lev",
        scatter_dimension=2,
        tiled=True,
    )
    pre_grad = pull_back(act_grad)[0].astype(jnp.bfloat16)
    padded_grad = extend(pre_grad)
    input_grad = backward_taps(padded_grad, conv_weight)
    conv_local = weight_taps(padded_input, pre_grad) * grid_scale
    join_local = (
        lax.dot_general(
            flat_all, flat_grad, (((0,), (0,)), ((), ())), preferred_element_type=jnp.float32
        ).reshape(lev_total, channels, lev_local, channels)
        * grid_scale
    )
    cycle_parts = (
        lax.psum_scatter(conv_local, "lon", scatter_dimension=3, tiled=True),
        lax.psum_scatter(join_local, "lon", scatter_dimension=1, tiled=True),
    )
    conv_grad, join_grad = lax.psum((cycle_parts[0], cycle_parts[1]), "lat")
    return (joined_fields, input_grad, conv_grad, join_grad)


def solution(mesh):
    in_specs = (
        P("lat", "lon", "lev", None),
        P("lev", None, None, None, None),
        P(),
        P("lat", "lon", "lev", None),
    )
    out_specs = (
        P("lat", "lon", "lev", None),
        P("lat", "lon", "lev", None),
        P("lev", None, None, "lon", None),
        P(None, "lon", "lev", None),
    )
    return jax.shard_map(
        per_device, mesh=mesh, in_specs=in_specs, out_specs=out_specs, check_vma=False
    )
```

profile of v0, /device:TPU:0, one launch (start us, length us, event | category | flops | bytes accessed | tf_op | source)
XLA Modules:
  0.0 420.6 jit_solution(4275923332570461178)
XLA Ops:
  8.7 6.1 %constant_dynamic-slice_fusion = bf16[8,192,4,192]{3,2,1,0:T(4,128)(2,1)} fusion(bf16[8,192,8,192]{3,2,1,0:T(8,128)(2,1)} %param.6, s32[]{:T(128)S(6)} %select_n.3), kind=kLoop, calls=%fused_computation.130 | loop fusion | bytes 4718596 | tf_op jit(solution)/shard_map/dynamic_slice | solution.py:91
  14.8 5.4 %reshape.56 = bf16[1536,768]{1,0:T(8,128)(2,1)S(1)} reshape(bf16[8,192,4,192]{3,2,1,0:T(4,128)(2,1)} %constant_dynamic-slice_fusion) | data formatting | bytes 4718592 | tf_op jit(solution)/shard_map/reshape | solution.py:91
  22.2 3.0 copy.75
  25.2 2.9 reshape.29
  28.1 3.6 copy.76
  33.0 3.1 collective-permute-start
  38.1 2.3 fusion.62
  45.8 2.3 collective-permute-done.3
  52.3 14.1 %reduce-scatter.4.cloned.1.call-done = f32[8,32,4,192]{3,1,0,2:T(8,128)} async-done(((f32[8,32,8,192]{3,1,0,2:T(8,128)}), f32[8,32,4,192]{3,1,0,2:T(8,128)}) %reduce-scatter.4.cloned.1.call-update) | async-done | bytes 786448 | tf_op jit(solution)/shard_map/reduce_scatter | solution.py:101
  66.4 2.8 fusion.21
  69.3 14.5 %all_gather.3 = bf16[8,32,8,192]{3,1,0,2:T(8,128)(2,1)S(1)} all-gather(bf16[8,32,4,192]{3,1,0,2:T(8,128)(2,1)S(1)} %get-tuple-element.19), channel_id=1, replica_groups=mesh['lon'=4,'lev'=2,'lat'=4] {'lev'}, dimensions={2}, use_global_device_ids=true | all-gather | bytes 1179648 | tf_op jit(solution)/shard_map/all_gather | solution.py:88
  85.4 2.7 reshape.30
  88.1 2.3 copy.80
  90.4 5.0 %broadcast_multiply_fusion = f32[8,192,4,192]{3,1,2,0:T(8,128)} fusion(bf16[8,192,256,1]{2,1,3,0:T(8,128)(2,1)} %bitcast.217, bf16[4,192,256,1]{2,1,0,3:T(8,128)(2,1)} %bitcast.220), kind=kOutput, calls=%fused_computation.1 | convolution fusion | flops 605159424 | bytes 5898240 | tf_op jit(solution)/shard_map/dot_general | solution.py:112
  100.8 3.5 maximum_multiply_fusion
  104.4 2.5 copy.106
  110.7 2.1 collective-permute-start.5
  112.8 2.9 fusion.22
  121.1 3.3 collective-permute-start.7
  130.1 77.6 %reduce-scatter.8.cloned.1.call-done = f32[8,48,4,192]{3,1,2,0:T(8,128)} async-done(((f32[8,192,4,192]{3,1,2,0:T(8,128)}), f32[8,48,4,192]{3,1,2,0:T(8,128)}) %reduce-scatter.8.cloned.1.call-update) | async-done | bytes 1179664 | tf_op jit(solution)/shard_map/reduce_scatter | solution.py:119
  207.7 126.4 %reduce-scatter.6.cloned.1.call-done = f32[4,3,3,48,192]{4,3,0,2,1:T(8,128)} async-done(((f32[4,3,3,192,192]{4,3,0,2,1:T(8,128)}), f32[4,3,3,48,192]{4,3,0,2,1:T(8,128)}) %reduce-scatter.6.cloned.1.call-update) | async-done | bytes 1327120 | tf_op jit(solution)/shard_map/reduce_scatter | solution.py:118
  342.0 67.0 %all-reduce.3.cloned.1.call-done = (f32[4,3,3,48,192]{4,3,0,2,1:T(8,128)}, f32[8,48,4,192]{3,1,2,0:T(8,128)}) async-done(((f32[4,3,3,48,192]{4,3,0,2,1:T(8,128)}, f32[8,48,4,192]{3,1,2,0:T(8,128)}), (f32[4,3,3,48,192]{4,3,0,2,1:T(8,128)}, f32[8,48,4,192]{3,1,2,0:T(8,128)})) %all-reduce.3.cloned.1.call-update) | async-done | bytes 2506768 | tf_op jit(solution)/shard_map/psum | solution.py:121
  409.0 2.9 copy.84
  411.9 2.2 copy.85
  (87 shorter events, 46.1 us)
Async XLA Ops:
  7.2 59.3 %reduce-scatter.4.cloned.1.call-start = ((), (), s32[]{:S(2)}) async-start(), calls=%async_computation.3 | async-start | bytes 3145728 | tf_op jit(solution)/shard_map/reduce_scatter | solution.py:101
  31.7 176.0 %reduce-scatter.8.cloned.1.call-start = ((), (), s32[]{:S(2)}) async-start(), calls=%async_computation.5 | async-start | bytes 7864320 | tf_op jit(solution)/shard_map/reduce_scatter | solution.py:119
  33.0 8.4 %collective-permute-start = (bf16[8,1,4,192]{3,1,0,2:T(2,128)(2,1)S(1)}, bf16[8,1,4,192]{3,1,0,2:T(2,128)(2,1)S(1)}, u32[]{:S(2)}, u32[]{:S(2)}) collective-permute-start(bf16[8,1,4,192]{3,1,0,2:T(2,128)(2,1)S(1)} %get-tuple-element.30), channel_id=1, source_target_pairs={{0,8},{8,16},{16,24},{24,0},{1,9},{9,17},{17,25},{25,1},{2,10},{10... | collective-permute-start | bytes 36872 | tf_op jit(solution)/shard_map/ppermute | solution.py:17
  36.0 5.3 %collective-permute-start.1 = (bf16[8,1,4,192]{3,1,0,2:T(2,128)(2,1)S(1)}, bf16[8,1,4,192]{3,1,0,2:T(2,128)(2,1)S(1)}, u32[]{:S(2)}, u32[]{:S(2)}) collective-permute-start(bf16[8,1,4,192]{3,1,0,2:T(2,128)(2,1)S(1)} %get-tuple-element.31), channel_id=1, source_target_pairs={{8,0},{16,8},{24,16},{0,24},{9,1},{17,9},{25,17},{1,25},{10,2},{18... | collective-permute-start | bytes 36872 | tf_op jit(solution)/shard_map/ppermute | solution.py:18
  41.3 7.2 %copy-start = (bf16[4,3,3,192,192]{4,3,2,1,0:T(8,128)(2,1)S(1)}, bf16[4,3,3,192,192]{4,3,2,1,0:T(8,128)(2,1)}, u32[]{:S(2)}) copy-start(bf16[4,3,3,192,192]{4,3,2,1,0:T(8,128)(2,1)} %param.5) | copy-start | bytes 7962628
  41.4 4.4 %collective-permute-start.2 = (bf16[1,34,4,192]{3,1,0,2:T(8,128)(2,1)S(1)}, bf16[1,34,4,192]{3,1,0,2:T(8,128)(2,1)S(1)}, u32[]{:S(2)}, u32[]{:S(2)}) collective-permute-start(bf16[1,34,4,192]{3,1,0,2:T(8,128)(2,1)S(1)} %get-tuple-element.26), channel_id=1, source_target_pairs={{0,1},{1,2},{2,3},{4,5},{5,6},{6,7},{8,9},{9,10},{10,11},{12,13},{... | collective-permute-start | bytes 156680 | tf_op jit(solution)/shard_map/ppermute | solution.py:17
  43.2 4.9 %collective-permute-start.3 = (bf16[1,34,4,192]{3,1,0,2:T(8,128)(2,1)S(1)}, bf16[1,34,4,192]{3,1,0,2:T(8,128)(2,1)S(1)}, u32[]{:S(2)}, u32[]{:S(2)}) collective-permute-start(bf16[1,34,4,192]{3,1,0,2:T(8,128)(2,1)S(1)} %get-tuple-element.27), channel_id=1, source_target_pairs={{1,0},{2,1},{3,2},{5,4},{6,5},{7,6},{9,8},{10,9},{11,10},{13,12},{... | collective-permute-start | bytes 156680 | tf_op jit(solution)/shard_map/ppermute | solution.py:18
  48.6 2.5 copy-start.4
  48.9 1.5 copy-start.8
  95.4 238.7 %reduce-scatter.6.cloned.1.call-start = ((), (), s32[]{:S(2)}) async-start(), calls=%async_computation.4 | async-start | bytes 8847360 | tf_op jit(solution)/shard_map/reduce_scatter | solution.py:118
  95.4 1.5 copy-start.5
  97.8 1.0 copy-start.11
  98.2 1.2 copy-start.3
  104.3 304.7 %all-reduce.3.cloned.1.call-start = ((), (), s32[]{:S(2)}) async-start(), calls=%async_computation.6 | async-start | bytes 6684672 | tf_op jit(solution)/shard_map/psum | solution.py:121
  108.9 9.7 %collective-permute-start.4 = (bf16[8,1,4,192]{3,1,0,2:T(2,128)(2,1)S(1)}, bf16[8,1,4,192]{3,1,0,2:T(2,128)(2,1)S(1)}, u32[]{:S(2)}, u32[]{:S(2)}) collective-permute-start(bf16[8,1,4,192]{3,1,0,2:T(2,128)(2,1)S(1)} %get-tuple-element.28), channel_id=1, source_target_pairs={{0,8},{8,16},{16,24},{24,0},{1,9},{9,17},{17,25},{25,1},{2,10},{10... | collective-permute-start | bytes 36872 | tf_op jit(solution)/shard_map/ppermute | solution.py:17
  110.7 9.1 %collective-permute-start.5 = (bf16[8,1,4,192]{3,1,0,2:T(2,128)(2,1)S(1)}, bf16[8,1,4,192]{3,1,0,2:T(2,128)(2,1)S(1)}, u32[]{:S(2)}, u32[]{:S(2)}) collective-permute-start(bf16[8,1,4,192]{3,1,0,2:T(2,128)(2,1)S(1)} %get-tuple-element.29), channel_id=1, source_target_pairs={{8,0},{16,8},{24,16},{0,24},{9,1},{17,9},{25,17},{1,25},{10,2},{18... | collective-permute-start | bytes 36872 | tf_op jit(solution)/shard_map/ppermute | solution.py:18
  112.8 2.9 copy-start.1
  119.8 5.9 %collective-permute-start.6 = (bf16[1,34,4,192]{3,1,0,2:T(8,128)(2,1)S(1)}, bf16[1,34,4,192]{3,1,0,2:T(8,128)(2,1)S(1)}, u32[]{:S(2)}, u32[]{:S(2)}) collective-permute-start(bf16[1,34,4,192]{3,1,0,2:T(8,128)(2,1)S(1)} %get-tuple-element.22), channel_id=1, source_target_pairs={{1,0},{2,1},{3,2},{5,4},{6,5},{7,6},{9,8},{10,9},{11,10},{13,12},{... | collective-permute-start | bytes 156680 | tf_op jit(solution)/shard_map/ppermute | solution.py:18
  121.1 4.6 %collective-permute-start.7 = (bf16[1,34,4,192]{3,1,0,2:T(8,128)(2,1)S(1)}, bf16[1,34,4,192]{3,1,0,2:T(8,128)(2,1)S(1)}, u32[]{:S(2)}, u32[]{:S(2)}) collective-permute-start(bf16[1,34,4,192]{3,1,0,2:T(8,128)(2,1)S(1)} %get-tuple-element.23), channel_id=1, source_target_pairs={{0,1},{1,2},{2,3},{4,5},{5,6},{6,7},{8,9},{9,10},{10,11},{12,13},{... | collective-permute-start | bytes 156680 | tf_op jit(solution)/shard_map/ppermute | solution.py:17
  334.1 2.9 copy-start.6
  334.1 2.9 copy-start.7
  334.2 2.9 copy-start.10
  337.0 1.9 copy-start.9
  409.0 2.9 copy-start.12
  (1 other events, 0.9 us)
Sparse Core Ops, SparseCore 0:
  31.8 34.5 reduce-scatter.3
  95.5 112.1 reduce-scatter.7
  210.1 123.9 reduce-scatter.5
  336.6 72.3 all-reduce.2
where the time goes:
time: 421 us
  waiting for transfers between devices  288 us (68%)
  local copies, waits for them, and re-layouts  45.5 us (11%)
  matrix products  35.9 us (9%)
  starting transfers between devices  16.8 us (4%)
  blocking collectives  14.5 us (3%)
  between operations  14.2 us (3%)
  other arithmetic  5.22 us (1%)
    reduce_scatter x1, waiting for transfers between devices, per_device(): lax.psum_scatter(conv_local, 'lon', scatter_dimension=3, tiled=True)  126 us
    reduce_scatter x1, waiting for transfers between devices, per_device(): lax.psum_scatter(join_local, 'lon', scatter_dimension=1, tiled=True)  77.6 us
    psum x1, waiting for transfers between devices, per_device(): conv_grad, join_grad = lax.psum((cycle_parts[0], cycle_parts[1]), 'lat')  67 us
    all_gather x1, blocking collectives, per_device(): all_levels = lax.all_gather(activation, 'lev', axis=2, tiled=True)  14.5 us
    reduce_scatter x1, waiting for transfers between devices, per_device(): lax.psum_scatter(partial_terms.reshape(lat_rows, lon_cols, lev_total, cha...  14.1 us
    dot_general x9, matrix products, backward_taps(): jnp.einsum('ablo,lio->abli', window, weight[:, tap_row, tap_col], preferr...  12.7 us
    unnamed x31, local copies, waits for them, and re-layouts  10.9 us
    ppermute x4, starting transfers between devices, extended(): before = lax.ppermute(last, axis, up)  9.8 us
  transfers between devices with their start and end apart: 12, of which 6 were waited for; matrix products, arithmetic and copies ran while one was open for 10% of the time, Pallas kernels for 0%

commit v1 on v0

v1 whole, which is shorter than its diff:
```python
import math

import jax
import jax.numpy as jnp
from jax import lax
from jax.experimental import pallas as pl
from jax.experimental.pallas import tpu as pltpu
from jax.sharding import PartitionSpec as P

F32 = jnp.float32
BF16 = jnp.bfloat16
MESH = pl.DeviceIdType.MESH
ROOT = math.sqrt(2.0 / math.pi)


def dot(a, b, a_dim, b_dim):
    return lax.dot_general(a, b, (((a_dim,), (b_dim,)), ((), ())), preferred_element_type=F32)


def make_kernel(n_lon, n_lat, rows, cols, levs, chans, scale):
    share = chans // n_lon
    cells = rows * cols
    wide = levs * chans

    def kernel(
        x_ref, cw_ref, jw_ref, jg_ref,
        jf_ref, ig_ref, gj_ref, gc_ref,
        jg_in, edge_out, edge_in, xs, ps, act, act_in, ag,
        own_a, s1_a, r1_a, s2_a, r2_a, s3_a, r3_a, g_a,
        own_b, s1_b, r1_b, s2_b, r2_b, s3_b, r3_b, g_b,
        own_c, s1_c, r1_c, s2_c, r2_c, s3_c, r3_c, g_c,
        lev_send, lev_recv, edge_send, edge_recv, lat_send, lat_recv,
        p1_send, p1_recv, p2_send, p2_recv, p3_send, p3_recv,
        p4_send, p4_recv, p5_send, p5_recv,
    ):
        z = lax.axis_index("lon")
        e = lax.axis_index("lev")
        t = lax.axis_index("lat")
        y = t // 2
        core = lax.rem(t, 2)
        right = lax.rem(z + 1, n_lon)
        left = lax.rem(z + n_lon - 1, n_lon)
        sibling = 2 * y + (1 - core)
        across = 2 * (1 - y) + core

        barrier = pltpu.get_barrier_semaphore()
        for d in range(1, n_lon):
            pl.semaphore_signal(
                barrier, inc=1, device_id={"lon": lax.rem(z + d, n_lon)}, device_id_type=MESH
            )
        for d in range(1, n_lat):
            pl.semaphore_signal(
                barrier, inc=1, device_id={"lat": lax.rem(t + d, n_lat)}, device_id_type=MESH
            )
        pl.semaphore_signal(barrier, inc=1, device_id={"lev": 1 - e}, device_id_type=MESH)
        pl.semaphore_wait(barrier, n_lon + n_lat - 1)

        def remote(src, dst, send, recv, where):
            return pltpu.make_async_remote_copy(
                src_ref=src, dst_ref=dst, send_sem=send, recv_sem=recv,
                device_id=where, device_id_type=MESH,
            )

        jg_copy = remote(jg_ref, jg_in, lev_send.at[0], lev_recv.at[0], {"lev": 1 - e})
        jg_copy.start()

        def edge_copies(n):
            return (
                remote(
                    edge_out.at[2 * n], edge_in.at[2 * n],
                    edge_send.at[2 * n], edge_recv.at[2 * n], {"lon": right},
                ),
                remote(
                    edge_out.at[2 * n + 1], edge_in.at[2 * n + 1],
                    edge_send.at[2 * n + 1], edge_recv.at[2 * n + 1], {"lon": left},
                ),
            )

        def put_middle(n, dst, l, value):
            edge_out[2 * n, l] = value[:, cols - 1, :]
            edge_out[2 * n + 1, l] = value[:, 0, :]
            dst[1 : rows + 1, 1, l] = value.astype(BF16)

        def put_sides(n, dst):
            @pl.loop(0, levs)
            def _(l):
                value = dst[1 : rows + 1, 1, l].astype(F32)
                before = edge_in[2 * n, l].reshape(rows, 1, chans)
                after = edge_in[2 * n + 1, l].reshape(rows, 1, chans)
                dst[1 : rows + 1, 0, l] = jnp.concatenate(
                    [before, value[:, : cols - 1]], axis=1
                ).astype(BF16)
                dst[1 : rows + 1, 2, l] = jnp.concatenate(
                    [value[:, 1:], after], axis=1
                ).astype(BF16)

        def lat_down(n, dst):
            return remote(
                dst.at[rows], dst.at[0], lat_send.at[2 * n], lat_recv.at[2 * n], {"lat": t + 1}
            )

        def lat_up(n, dst):
            return remote(
                dst.at[1], dst.at[rows + 1],
                lat_send.at[2 * n + 1], lat_recv.at[2 * n + 1], {"lat": t - 1},
            )

        def lat_start(n, dst):
            @pl.when(t < n_lat - 1)
            def _():
                lat_down(n, dst).start()

            @pl.when(t > 0)
            def _():
                lat_up(n, dst).start()

            @pl.when(t == 0)
            def _():
                dst[0] = jnp.zeros(dst.shape[1:], BF16)

            @pl.when(t == n_lat - 1)
            def _():
                dst[rows + 1] = jnp.zeros(dst.shape[1:], BF16)

        def lat_wait(n, dst):
            @pl.when(t < n_lat - 1)
            def _():
                lat_down(n, dst).wait_send()
                lat_up(n, dst).wait_recv()

            @pl.when(t > 0)
            def _():
                lat_up(n, dst).wait_send()
                lat_down(n, dst).wait_recv()

        @pl.loop(0, levs)
        def _(l):
            put_middle(0, xs, l, x_ref[l].astype(F32))

        edges = edge_copies(0)
        for c in edges:
            c.start()

        @pl.loop(0, levs)
        def _(l):
            block = jw_ref[e * levs + l, :, pl.ds(pl.multiple_of(e * wide, 128), wide)]
            ag[l] = dot(jg_ref[...], block, 1, 1)

        for c in edges:
            c.wait()
        put_sides(0, xs)
        lat_start(0, xs)

        jg_copy.wait()

        @pl.loop(0, levs)
        def _(l):
            block = jw_ref[e * levs + l, :, pl.ds(pl.multiple_of((1 - e) * wide, 128), wide)]
            ag[l] += dot(jg_in[...], block, 1, 1)

        lat_wait(0, xs)

        @pl.loop(0, levs)
        def _(l):
            total = None
            for p in range(3):
                for q in range(3):
                    window = xs[p : p + rows, q, l].reshape(cells, chans)
                    term = dot(window, cw_ref[l, p, q], 1, 0)
                    total = term if total is None else total + term
            square = total * total
            bent = jnp.tanh(ROOT * (total + 0.044715 * total * square))
            half = 0.5 * (1.0 + bent)
            act[l] = (total * half).astype(BF16)
            slope = half + 0.5 * total * (1.0 - bent * bent) * (
                ROOT * (1.0 + 3.0 * 0.044715 * square)
            )
            grad = (ag[l] * slope).astype(BF16).astype(F32)
            put_middle(1, ps, l, grad.reshape(rows, cols, chans))

        act_copy = remote(act, act_in, lev_send.at[1], lev_recv.at[1], {"lev": 1 - e})
        act_copy.start()
        edges_g = edge_copies(1)
        for c in edges_g:
            c.start()

        class Round:
            def __init__(self, n, bufs):
                self.n = n
                self.own, self.s1, self.r1, self.s2, self.r2, self.s3, self.r3, self.g = bufs
                n3 = n * (n_lon - 1)
                self.c1 = remote(
                    self.s1, self.r1, p1_send.at[n], p1_recv.at[n], {"lat": sibling}
                )
                self.c2 = remote(
                    self.s2, self.r2, p2_send.at[n], p2_recv.at[n], {"lat": across}
                )
                self.c3 = [
                    remote(
                        self.s3.at[d - 1], self.r3.at[d - 1],
                        p3_send.at[n3 + d - 1], p3_recv.at[n3 + d - 1],
                        {"lon": lax.rem(z + d, n_lon)},
                    )
                    for d in range(1, n_lon)
                ]
                self.c4 = remote(
                    self.g.at[y, core], self.g.at[y, core],
                    p4_send.at[n], p4_recv.at[n], {"lat": across},
                )
                self.c5 = [
                    remote(
                        self.g.at[h, core], self.g.at[h, core],
                        p5_send.at[2 * n + h], p5_recv.at[2 * n + h], {"lat": sibling},
                    )
                    for h in range(2)
                ]

            def first(self, fill):
                @pl.loop(0, 2)
                def _(k):
                    fill(2 * k + (1 - core), self.s1, k, BF16)

                self.c1.start()

                @pl.loop(0, 2)
                def _(k):
                    fill(2 * k + core, self.own, k, F32)

            def second(self):
                self.c1.wait()

                @pl.loop(0, n_lon)
                def _(q):
                    self.s2[q] = (self.own[1 - y, q] + self.r1[1 - y, q].astype(F32)).astype(BF16)

                self.c2.start()

                @pl.loop(0, n_lon)
                def _(q):
                    self.own[y, q] += self.r1[y, q].astype(F32)

            def third(self):
                self.c2.wait()
                for d in range(1, n_lon):
                    q = lax.rem(z + d, n_lon)
                    self.s3[d - 1] = (self.own[y, q] + self.r2[q].astype(F32)).astype(BF16)
                    self.c3[d - 1].start()

            def fourth(self):
                total = self.own[y, z] + self.r2[z].astype(F32)
                for d in range(1, n_lon):
                    self.c3[d - 1].wait()
                    total = total + self.r3[d - 1].astype(F32)
                self.g[y, core] = total * scale
                self.c4.start()

            def fifth(self):
                self.c4.wait()
                for c in self.c5:
                    c.start()

            def finish(self, put):
                for c in self.c5:
                    c.wait()
                for h in range(2):
                    for k in range(2):
                        put(2 * h + k, self.g[h, k])

        def spread(value, dst, k, dtype, lanes):
            for q in range(n_lon):
                dst[k, q, :, lanes] = value[q * share : (q + 1) * share].astype(dtype)

        def fill_own(l, dst, k, dtype):
            spread(dot(act[l], jg_ref[...], 0, 0), dst, k, dtype, slice(None))

        def fill_other(l, dst, k, dtype):
            spread(dot(act_in[l], jg_ref[...], 0, 0), dst, k, dtype, slice(None))

        def fill_conv(l, dst, k, dtype):
            grad = ps[1 : rows + 1, 1, l].reshape(cells, chans)
            for p in range(3):
                for q in range(3):
                    window = xs[p : p + rows, q, l].reshape(cells, chans)
                    tap = 3 * p + q
                    spread(
                        dot(window, grad, 0, 0), dst, k, dtype,
                        slice(tap * chans, (tap + 1) * chans),
                    )

        ra = Round(0, (own_a, s1_a, r1_a, s2_a, r2_a, s3_a, r3_a, g_a))
        rb = Round(1, (own_b, s1_b, r1_b, s2_b, r2_b, s3_b, r3_b, g_b))
        rc = Round(2, (own_c, s1_c, r1_c, s2_c, r2_c, s3_c, r3_c, g_c))

        ra.first(fill_own)
        rc.first(fill_conv)
        ra.second()
        for c in edges_g:
            c.wait()
        put_sides(1, ps)
        lat_start(1, ps)
        rc.second()
        act_copy.wait()
        rb.first(fill_other)
        ra.third()
        rb.second()
        lat_wait(1, ps)

        @pl.loop(0, levs)
        def _(l):
            total = None
            for p in range(3):
                for q in range(3):
                    window = ps[2 - p : 2 - p + rows, 2 - q, l].reshape(cells, chans)
                    term = dot(window, cw_ref[l, p, q], 1, 1)
                    total = term if total is None else total + term
            ig_ref[l] = total

        rc.third()
        own_cols = pl.ds(pl.multiple_of(e * wide, 128), wide)
        jf_ref[...] = jnp.zeros(jf_ref.shape, F32)

        @pl.loop(0, levs)
        def _(l):
            jf_ref[...] += dot(act[l], jw_ref[e * levs + l, :, own_cols], 1, 0)

        ra.fourth()
        rb.third()

        @pl.loop(0, levs)
        def _(l):
            jf_ref[...] += dot(act_in[l], jw_ref[(1 - e) * levs + l, :, own_cols], 1, 0)

        rc.fourth()
        ra.fifth()
        rb.fourth()
        rc.fifth()
        rb.fifth()

        def put_join(half):
            def put(i, value):
                gj_ref[half, i] = value

            return put

        def put_conv(i, value):
            gc_ref[i] = value

        ra.finish(put_join(e))
        rc.finish(put_conv)
        rb.finish(put_join(1 - e))

    def round_scratch(width):
        block = (n_lon, share, width)
        return [
            pltpu.VMEM((2,) + block, F32),
            pltpu.VMEM((2,) + block, BF16),
            pltpu.VMEM((2,) + block, BF16),
            pltpu.VMEM(block, BF16),
            pltpu.VMEM(block, BF16),
            pltpu.VMEM((n_lon - 1, share, width), BF16),
            pltpu.VMEM((n_lon - 1, share, width), BF16),
            pltpu.VMEM((2, 2, share, width), F32),
        ]

    dma = pltpu.SemaphoreType.DMA
    scratch = [
        pltpu.VMEM((cells, wide), BF16),
        pltpu.VMEM((4, levs, rows, chans), F32),
        pltpu.VMEM((4, levs, rows, chans), F32),
        pltpu.VMEM((rows + 2, 3, levs, cols, chans), BF16),
        pltpu.VMEM((rows + 2, 3, levs, cols, chans), BF16),
        pltpu.VMEM((levs, cells, chans), BF16),
        pltpu.VMEM((levs, cells, chans), BF16),
        pltpu.VMEM((levs, cells, chans), F32),
        *round_scratch(wide),
        *round_scratch(wide),
        *round_scratch(9 * chans),
        dma((2,)), dma((2,)), dma((4,)), dma((4,)), dma((4,)), dma((4,)),
        dma((3,)), dma((3,)), dma((3,)), dma((3,)),
        dma((3 * (n_lon - 1),)), dma((3 * (n_lon - 1),)),
        dma((3,)), dma((3,)), dma((6,)), dma((6,)),
    ]
    vmem = pl.BlockSpec(memory_space=pltpu.VMEM)
    return pl.pallas_call(
        kernel,
        out_shape=(
            jax.ShapeDtypeStruct((cells, wide), F32),
            jax.ShapeDtypeStruct((levs, cells, chans), F32),
            jax.ShapeDtypeStruct((2, levs, share, wide), F32),
            jax.ShapeDtypeStruct((levs, share, 9 * chans), F32),
        ),
        in_specs=[vmem] * 4,
        out_specs=(vmem,) * 4,
        scratch_shapes=scratch,
        compiler_params=pltpu.CompilerParams(
            collective_id=0, has_side_effects=True, vmem_limit_bytes=60 * 1024 * 1024
        ),
    )


def per_device(features, conv_weight, join_weight, joined_grad):
    rows, cols, levs, chans = features.shape
    lev_total = join_weight.shape[0]
    n_lon, n_lat = lax.axis_size("lon"), lax.axis_size("lat")
    share = chans // n_lon
    scale = 1.0 / math.sqrt(rows * n_lat * cols * n_lon)
    run = make_kernel(n_lon, n_lat, rows, cols, levs, chans, scale)
    jf, ig, gj, gc = run(
        jnp.transpose(features, (2, 0, 1, 3)),
        conv_weight,
        join_weight.reshape(lev_total, chans, lev_total * chans),
        joined_grad.reshape(rows * cols, levs * chans),
    )
    return (
        jf.reshape(features.shape),
        jnp.transpose(ig.reshape(levs, rows, cols, chans), (1, 2, 0, 3)),
        jnp.transpose(gc.reshape(levs, share, 3, 3, chans), (0, 2, 3, 1, 4)),
        gj.reshape(lev_total, share, levs, chans),
    )


def solution(mesh):
    in_specs = (
        P("lat", "lon", "lev", None),
        P("lev", None, None, None, None),
        P(),
        P("lat", "lon", "lev", None),
    )
    out_specs = (
        P("lat", "lon", "lev", None),
        P("lat", "lon", "lev", None),
        P("lev", None, None, "lon", None),
        P(None, "lon", "lev", None),
    )
    return jax.shard_map(
        per_device, mesh=mesh, in_specs=in_specs, out_specs=out_specs, check_vma=False
    )
```

time: 421 us -> 113 us (0.27)
  the two profiles are of different devices: /device:TPU:0 before, /device:TPU:9 now
where the time goes in v1:
time: 113 us; the launch traced here: 112 us
  Pallas kernels  85.4 us (76%)
  local copies, waits for them, and re-layouts  26.2 us (23%)
    pallas_call x1, Pallas kernels, per_device(): run(jnp.transpose(features, (2, 0, 1, 3)), conv_weight, join_weight.resha...  85.4 us
    reshape x1, local copies, waits for them, and re-layouts, per_device(): join_weight.reshape(lev_total, chans, lev_total * chans)  10.5 us
    unnamed x6, local copies, waits for them, and re-layouts  3.45 us
    reshape x1, local copies, waits for them, and re-layouts, per_device(): ig.reshape(levs, rows, cols, chans)  3.01 us
    reshape x1, local copies, waits for them, and re-layouts, per_device(): gc.reshape(levs, share, 3, 3, chans)  2.92 us
    reshape x1, local copies, waits for them, and re-layouts, per_device(): gj.reshape(lev_total, share, levs, chans)  2.29 us

profile of v1, /device:TPU:9, one launch (start us, length us, event | category | flops | bytes accessed | tf_op | source)
XLA Modules:
  0.0 112.3 jit_solution(16105194746208171073)
XLA Ops:
  0.6 2.3 %reshape.27.jg_ref = bf16[256,768]{1,0:T(8,128)(2,1)} reshape(bf16[8,32,4,192]{3,2,1,0:T(4,128)(2,1)} %param.7) | data formatting | bytes 786432 | tf_op jit(solution)/shard_map/reshape | solution.py:412
  2.9 1.9 %copy.17 = bf16[8,32,4,192]{3,1,0,2:T(8,128)(2,1)} copy(bf16[8,32,4,192]{3,2,1,0:T(4,128)(2,1)} %param.4) | data formatting | bytes 786432 | tf_op args[0]
  4.8 10.5 %reshape.26.jw_ref = bf16[8,192,1536]{2,1,0:T(8,128)(2,1)} reshape(bf16[8,192,8,192]{3,2,1,0:T(8,128)(2,1)} %param.6) | data formatting | bytes 9437184 | tf_op jit(solution)/shard_map/reshape | solution.py:411
  15.3 85.4 %shard_map.75 = (f32[256,768]{1,0:T(8,128)}, f32[4,256,192]{2,1,0:T(8,128)}, f32[2,4,48,768]{3,2,1,0:T(8,128)}, f32[4,48,1728]{2,1,0:T(8,128)}) custom-call(bf16[4,8,32,192]{3,2,1,0:T(8,128)(2,1)} %bitcast.13, bf16[4,3,3,192,192]{4,3,2,1,0:T(8,128)(2,1)} %cw_ref.1, bf16[8,192,1536]{2,1,0:T(8,128)(2,1)} %reshape.26.jw_ref, bf16[256,768]{1,0:T(8,128)(2,1)} %reshape.27.jg_ref), custom_call_target="tpu_custom_call" | custom-call | tf_op jit(solution)/shard_map/pallas_call | solution.py:408
  100.8 0.0 copy-start.1
  100.8 0.0 copy-start
  100.8 3.0 %copy.16 = f32[4,8,32,192]{3,0,2,1:T(4,128)} copy(f32[4,8,32,192]{3,2,1,0:T(8,128)} %bitcast.15) | data formatting | bytes 1572864 | tf_op jit(solution)/shard_map/reshape | solution.py:416
  103.8 0.0 copy-done.1
  103.8 1.7 %reshape.28 = f32[8,32,4,192]{3,2,1,0:T(4,128)} reshape(f32[256,768]{1,0:T(8,128)S(1)} %copy-done.1) | data formatting | bytes 1572864 | tf_op jit(solution)/shard_map/reshape | solution.py:415
  105.5 0.0 copy-done
  105.5 2.3 %reshape.31 = f32[8,48,4,192]{3,2,1,0:T(4,128)} reshape(f32[2,4,48,768]{3,2,1,0:T(8,128)S(1)} %copy-done) | data formatting | bytes 2359296 | tf_op jit(solution)/shard_map/reshape | solution.py:418
  107.8 2.9 %reshape.30 = f32[4,48,3,3,192]{4,3,2,1,0:T(4,128)S(1)} reshape(f32[4,48,1728]{2,1,0:T(8,128)} %get-tuple-element.10) | data formatting | bytes 2654208 | tf_op jit(solution)/shard_map/reshape | solution.py:417
  110.8 1.5 %copy.13 = f32[4,3,3,48,192]{4,3,2,1,0:T(8,128)} copy(f32[4,3,3,48,192]{4,2,1,3,0:T(4,128)S(1)} %bitcast.12) | data formatting | bytes 2654208
Async XLA Ops:
  100.8 3.0 %copy-start.1 = (f32[256,768]{1,0:T(8,128)S(1)}, f32[256,768]{1,0:T(8,128)}, u32[]{:S(2)}) copy-start(f32[256,768]{1,0:T(8,128)} %get-tuple-element.8) | copy-start | bytes 2359300
  100.8 4.8 %copy-start = (f32[2,4,48,768]{3,2,1,0:T(8,128)S(1)}, f32[2,4,48,768]{3,2,1,0:T(8,128)}, u32[]{:S(2)}) copy-start(f32[2,4,48,768]{3,2,1,0:T(8,128)} %get-tuple-element.11) | copy-start | bytes 3538948

commit v2 on v1

--- a/solution.py
+++ b/solution.py
@@ -23,12 +23,13 @@
     wide = levs * chans
 
     def kernel(
-        x_ref, cw_ref, jw_ref, jg_ref,
+        x_ref, cw_ref, raw_ref, jg_ref,
         jf_ref, ig_ref, gj_ref, gc_ref,
         jg_in, edge_out, edge_in, xs, ps, act, act_in, ag,
         own_a, s1_a, r1_a, s2_a, r2_a, s3_a, r3_a, g_a,
         own_b, s1_b, r1_b, s2_b, r2_b, s3_b, r3_b, g_b,
         own_c, s1_c, r1_c, s2_c, r2_c, s3_c, r3_c, g_c,
+        jw_ref, raw, loose, fields, jw_sem,
         lev_send, lev_recv, edge_send, edge_recv, lat_send, lat_recv,
         p1_send, p1_recv, p2_send, p2_recv, p3_send, p3_recv,
         p4_send, p4_recv, p5_send, p5_recv,
@@ -43,6 +44,29 @@
         sibling = 2 * y + (1 - core)
         across = 2 * (1 - y) + core
 
+        def jw_copy(l):
+            return pltpu.make_async_copy(raw_ref.at[l], raw.at[l], jw_sem.at[l])
+
+        @pl.loop(0, levs)
+        def _(l):
+            jw_copy(e * levs + l).start()
+
+        @pl.loop(0, levs)
+        def _(l):
+            jw_copy((1 - e) * levs + l).start()
+
+        def order_join(l):
+            jw_copy(l).wait()
+            for n, low in enumerate(range(0, chans, 128)):
+                count = min(128, chans - low)
+                loose[n, :, :count] = raw[l, :, low : low + count].astype(F32)
+            for m in range(2 * levs):
+                for n, low in enumerate(range(0, chans, 128)):
+                    count = min(128, chans - low)
+                    piece = loose.at[n][pl.ds(m, chans, stride=2 * levs), :]
+                    first = m * chans + low
+                    jw_ref[l, :, first : first + count] = piece[:, :count].astype(BF16)
+
         barrier = pltpu.get_barrier_semaphore()
         for d in range(1, n_lon):
             pl.semaphore_signal(
@@ -143,6 +167,7 @@
 
         @pl.loop(0, levs)
         def _(l):
+            order_join(e * levs + l)
             block = jw_ref[e * levs + l, :, pl.ds(pl.multiple_of(e * wide, 128), wide)]
             ag[l] = dot(jg_ref[...], block, 1, 1)
 
@@ -313,22 +338,33 @@
                     window = ps[2 - p : 2 - p + rows, 2 - q, l].reshape(cells, chans)
                     term = dot(window, cw_ref[l, p, q], 1, 1)
                     total = term if total is None else total + term
-            ig_ref[l] = total
+            ag[l] = total
+
+        for l in range(levs):
+            ig_ref[:, l, :] = ag[l]
 
         rc.third()
         own_cols = pl.ds(pl.multiple_of(e * wide, 128), wide)
-        jf_ref[...] = jnp.zeros(jf_ref.shape, F32)
-
-        @pl.loop(0, levs)
-        def _(l):
-            jf_ref[...] += dot(act[l], jw_ref[e * levs + l, :, own_cols], 1, 0)
+
+        @pl.loop(0, levs)
+        def _(l):
+            order_join((1 - e) * levs + l)
+
+        fields[...] = jnp.zeros(fields.shape, F32)
+
+        @pl.loop(0, levs)
+        def _(l):
+            fields[...] += dot(act[l], jw_ref[e * levs + l, :, own_cols], 1, 0)
 
         ra.fourth()
         rb.third()
 
         @pl.loop(0, levs)
         def _(l):
-            jf_ref[...] += dot(act_in[l], jw_ref[(1 - e) * levs + l, :, own_cols], 1, 0)
+            fields[...] += dot(act_in[l], jw_ref[(1 - e) * levs + l, :, own_cols], 1, 0)
+
+        for m in range(levs):
+            jf_ref[:, m, :] = fields[:, m * chans : (m + 1) * chans]
 
         rc.fourth()
         ra.fifth()
@@ -338,12 +374,14 @@
 
         def put_join(half):
             def put(i, value):
-                gj_ref[half, i] = value
+                for m in range(levs):
+                    gj_ref[half, i, :, m, :] = value[:, m * chans : (m + 1) * chans]
 
             return put
 
         def put_conv(i, value):
-            gc_ref[i] = value
+            for tap in range(9):
+                gc_ref[i, tap // 3, tap % 3] = value[:, tap * chans : (tap + 1) * chans]
 
         ra.finish(put_join(e))
         rc.finish(put_conv)
@@ -375,6 +413,11 @@
         *round_scratch(wide),
         *round_scratch(wide),
         *round_scratch(9 * chans),
+        pltpu.VMEM((2 * levs, chans, 2 * wide), BF16),
+        pltpu.VMEM((2 * levs, 2 * wide, chans), BF16),
+        pltpu.VMEM((pl.cdiv(chans, 128), 2 * wide, 128), F32),
+        pltpu.VMEM((cells, wide), F32),
+        dma((2 * levs,)),
         dma((2,)), dma((2,)), dma((4,)), dma((4,)), dma((4,)), dma((4,)),
         dma((3,)), dma((3,)), dma((3,)), dma((3,)),
         dma((3 * (n_lon - 1),)), dma((3 * (n_lon - 1),)),
@@ -384,12 +427,12 @@
     return pl.pallas_call(
         kernel,
         out_shape=(
-            jax.ShapeDtypeStruct((cells, wide), F32),
-            jax.ShapeDtypeStruct((levs, cells, chans), F32),
-            jax.ShapeDtypeStruct((2, levs, share, wide), F32),
-            jax.ShapeDtypeStruct((levs, share, 9 * chans), F32),
+            jax.ShapeDtypeStruct((cells, levs, chans), F32),
+            jax.ShapeDtypeStruct((cells, levs, chans), F32),
+            jax.ShapeDtypeStruct((2, levs, share, levs, chans), F32),
+            jax.ShapeDtypeStruct((levs, 3, 3, share, chans), F32),
         ),
-        in_specs=[vmem] * 4,
+        in_specs=[vmem, vmem, pl.BlockSpec(memory_space=pl.ANY), vmem],
         out_specs=(vmem,) * 4,
         scratch_shapes=scratch,
         compiler_params=pltpu.CompilerParams(
@@ -408,13 +451,13 @@
     jf, ig, gj, gc = run(
         jnp.transpose(features, (2, 0, 1, 3)),
         conv_weight,
-        join_weight.reshape(lev_total, chans, lev_total * chans),
+        join_weight.reshape(lev_total, chans * lev_total, chans),
         joined_grad.reshape(rows * cols, levs * chans),
     )
     return (
         jf.reshape(features.shape),
-        jnp.transpose(ig.reshape(levs, rows, cols, chans), (1, 2, 0, 3)),
-        jnp.transpose(gc.reshape(levs, share, 3, 3, chans), (0, 2, 3, 1, 4)),
+        ig.reshape(features.shape),
+        gc,
         gj.reshape(lev_total, share, levs, chans),
     )
 

time: 113 us -> 96.1 us (0.85)
  local copies, waits for them, and re-layouts: 26.2 us -> 10.9 us
    reshape x5 -> x0, local copies, waits for them, and re-layouts: 20.5 us -> none  [the longest x1 10.5 us: per_device(): join_weight.reshape(lev_total, chans, lev_total * chans)]
    unnamed x6 -> x11, local copies, waits for them, and re-layouts: 3.45 us -> 8.62 us
where the time goes in v2:
time: 96.1 us; the launch traced here: 95.9 us
  Pallas kernels  84.3 us (88%)
  local copies, waits for them, and re-layouts  10.9 us (11%)
    pallas_call x1, Pallas kernels, per_device(): run(jnp.transpose(features, (2, 0, 1, 3)), conv_weight, join_weight.resha...  84.3 us
    unnamed x11, local copies, waits for them, and re-layouts  8.62 us
    reshape x1, local copies, waits for them, and re-layouts, per_device(): joined_grad.reshape(rows * cols, levs * chans)  2.25 us

profile of v2, /device:TPU:9, one launch (start us, length us, event | category | flops | bytes accessed | tf_op | source)
XLA Modules:
  0.0 95.9 jit_solution(8276065567180747738)
XLA Ops:
  0.6 2.3 %reshape.24.jg_ref = bf16[256,768]{1,0:T(8,128)(2,1)} reshape(bf16[8,32,4,192]{3,2,1,0:T(4,128)(2,1)} %param.7) | data formatting | bytes 786432 | tf_op jit(solution)/shard_map/reshape | solution.py:455
  2.9 1.9 %copy.10 = bf16[8,32,4,192]{3,1,0,2:T(8,128)(2,1)} copy(bf16[8,32,4,192]{3,2,1,0:T(4,128)(2,1)} %param.4) | data formatting | bytes 786432 | tf_op args[0]
  4.8 84.3 %shard_map.75 = (f32[256,4,192]{2,1,0:T(4,128)}, f32[256,4,192]{2,1,0:T(4,128)}, f32[2,4,48,4,192]{4,3,2,1,0:T(4,128)}, f32[4,3,3,48,192]{4,3,2,1,0:T(8,128)}) custom-call(bf16[4,8,32,192]{3,2,1,0:T(8,128)(2,1)} %bitcast.8, bf16[4,3,3,192,192]{4,3,2,1,0:T(8,128)(2,1)} %cw_ref.1, bf16[8,1536,192]{2,1,0:T(8,128)(2,1)} %bitcast.7, bf16[256,768]{1,0:T(8,128)(2,1)} %reshape.24.jg_ref), custom_call_target="tpu_custom_call" | custom-call | tf_op jit(solution)/shard_map/pallas_call | solution.py:451
  89.2 0.0 copy-start.2
  89.2 0.0 copy-start
  89.2 2.5 %copy.15 = f32[8,32,4,192]{3,2,1,0:T(4,128)} copy(f32[8,32,4,192]{3,2,1,0:T(4,128)} %bitcast.11) | data formatting | bytes 1572864
  91.7 0.0 copy-done.2
  91.7 1.0 %copy.16 = f32[8,32,4,192]{3,2,1,0:T(4,128)} copy(f32[8,32,4,192]{3,2,1,0:T(4,128)S(1)} %bitcast.10) | data formatting | bytes 1572864
  92.7 0.0 copy-done
  92.7 0.0 copy-start.1
  92.7 1.2 %copy.17 = f32[4,3,3,48,192]{4,3,2,1,0:T(8,128)} copy(f32[4,3,3,48,192]{4,3,2,1,0:T(8,128)S(1)} %copy-done) | data formatting | bytes 2654208
  93.9 0.8 copy-done.1
  94.7 1.1 %copy.18 = f32[8,48,4,192]{3,2,1,0:T(4,128)} copy(f32[8,48,4,192]{3,2,1,0:T(4,128)S(1)} %bitcast.9) | data formatting | bytes 2359296
Async XLA Ops:
  89.2 2.5 %copy-start.2 = (f32[256,4,192]{2,1,0:T(4,128)S(1)}, f32[256,4,192]{2,1,0:T(4,128)}, u32[]{:S(2)}) copy-start(f32[256,4,192]{2,1,0:T(4,128)} %get-tuple-element.9) | copy-start | bytes 2359300
  89.2 3.5 %copy-start = (f32[4,3,3,48,192]{4,3,2,1,0:T(8,128)S(1)}, f32[4,3,3,48,192]{4,3,2,1,0:T(8,128)}, u32[]{:S(2)}) copy-start(f32[4,3,3,48,192]{4,3,2,1,0:T(8,128)} %get-tuple-element.18) | copy-start | bytes 3981316
  92.7 2.0 %copy-start.1 = (f32[2,4,48,4,192]{4,3,2,1,0:T(4,128)S(1)}, f32[2,4,48,4,192]{4,3,2,1,0:T(4,128)}, u32[]{:S(2)}) copy-start(f32[2,4,48,4,192]{4,3,2,1,0:T(4,128)} %get-tuple-element.11) | copy-start | bytes 3538948

commit v3 on v2

--- a/solution.py
+++ b/solution.py
@@ -10,6 +10,7 @@
 F32 = jnp.float32
 BF16 = jnp.bfloat16
 MESH = pl.DeviceIdType.MESH
+FIRST_TAPS = 4
 ROOT = math.sqrt(2.0 / math.pi)
 
 
@@ -29,7 +30,8 @@
         own_a, s1_a, r1_a, s2_a, r2_a, s3_a, r3_a, g_a,
         own_b, s1_b, r1_b, s2_b, r2_b, s3_b, r3_b, g_b,
         own_c, s1_c, r1_c, s2_c, r2_c, s3_c, r3_c, g_c,
-        jw_ref, raw, loose, fields, jw_sem,
+        own_d, s1_d, r1_d, s2_d, r2_d, s3_d, r3_d, g_d,
+        jw_ref, raw, loose, fields, slopes, jw_sem,
         lev_send, lev_recv, edge_send, edge_recv, lat_send, lat_recv,
         p1_send, p1_recv, p2_send, p2_recv, p3_send, p3_recv,
         p4_send, p4_recv, p5_send, p5_recv,
@@ -168,20 +170,16 @@
         @pl.loop(0, levs)
         def _(l):
             order_join(e * levs + l)
-            block = jw_ref[e * levs + l, :, pl.ds(pl.multiple_of(e * wide, 128), wide)]
-            ag[l] = dot(jg_ref[...], block, 1, 1)
 
         for c in edges:
             c.wait()
         put_sides(0, xs)
         lat_start(0, xs)
 
-        jg_copy.wait()
-
-        @pl.loop(0, levs)
-        def _(l):
-            block = jw_ref[e * levs + l, :, pl.ds(pl.multiple_of((1 - e) * wide, 128), wide)]
-            ag[l] += dot(jg_in[...], block, 1, 1)
+        @pl.loop(0, levs)
+        def _(l):
+            block = jw_ref[e * levs + l, :, pl.ds(pl.multiple_of(e * wide, 128), wide)]
+            ag[l] = dot(jg_ref[...], block, 1, 1)
 
         lat_wait(0, xs)
 
@@ -197,17 +195,12 @@
             bent = jnp.tanh(ROOT * (total + 0.044715 * total * square))
             half = 0.5 * (1.0 + bent)
             act[l] = (total * half).astype(BF16)
-            slope = half + 0.5 * total * (1.0 - bent * bent) * (
+            slopes[l] = half + 0.5 * total * (1.0 - bent * bent) * (
                 ROOT * (1.0 + 3.0 * 0.044715 * square)
             )
-            grad = (ag[l] * slope).astype(BF16).astype(F32)
-            put_middle(1, ps, l, grad.reshape(rows, cols, chans))
 
         act_copy = remote(act, act_in, lev_send.at[1], lev_recv.at[1], {"lev": 1 - e})
         act_copy.start()
-        edges_g = edge_copies(1)
-        for c in edges_g:
-            c.start()
 
         class Round:
             def __init__(self, n, bufs):
@@ -301,33 +294,57 @@
         def fill_other(l, dst, k, dtype):
             spread(dot(act_in[l], jg_ref[...], 0, 0), dst, k, dtype, slice(None))
 
-        def fill_conv(l, dst, k, dtype):
-            grad = ps[1 : rows + 1, 1, l].reshape(cells, chans)
-            for p in range(3):
-                for q in range(3):
-                    window = xs[p : p + rows, q, l].reshape(cells, chans)
-                    tap = 3 * p + q
+        def fill_taps(taps):
+            def fill(l, dst, k, dtype):
+                grad = ps[1 : rows + 1, 1, l].reshape(cells, chans)
+                for n, tap in enumerate(taps):
+                    window = xs[tap // 3 : tap // 3 + rows, tap % 3, l].reshape(cells, chans)
                     spread(
                         dot(window, grad, 0, 0), dst, k, dtype,
-                        slice(tap * chans, (tap + 1) * chans),
+                        slice(n * chans, (n + 1) * chans),
                     )
+
+            return fill
 
         ra = Round(0, (own_a, s1_a, r1_a, s2_a, r2_a, s3_a, r3_a, g_a))
         rb = Round(1, (own_b, s1_b, r1_b, s2_b, r2_b, s3_b, r3_b, g_b))
         rc = Round(2, (own_c, s1_c, r1_c, s2_c, r2_c, s3_c, r3_c, g_c))
+        rd = Round(3, (own_d, s1_d, r1_d, s2_d, r2_d, s3_d, r3_d, g_d))
 
         ra.first(fill_own)
-        rc.first(fill_conv)
         ra.second()
+        jg_copy.wait()
+
+        @pl.loop(0, levs)
+        def _(l):
+            block = jw_ref[e * levs + l, :, pl.ds(pl.multiple_of((1 - e) * wide, 128), wide)]
+            total = ag[l] + dot(jg_in[...], block, 1, 1)
+            grad = (total * slopes[l]).astype(BF16).astype(F32)
+            put_middle(1, ps, l, grad.reshape(rows, cols, chans))
+
+        edges_g = edge_copies(1)
+        for c in edges_g:
+            c.start()
+
+        rc.first(fill_taps(range(FIRST_TAPS)))
+        rc.second()
         for c in edges_g:
             c.wait()
         put_sides(1, ps)
         lat_start(1, ps)
-        rc.second()
+        rd.first(fill_taps(range(FIRST_TAPS, 9)))
+        ra.third()
+        rd.second()
         act_copy.wait()
         rb.first(fill_other)
-        ra.third()
+        rc.third()
         rb.second()
+
+        @pl.loop(0, levs)
+        def _(l):
+            order_join((1 - e) * levs + l)
+
+        ra.fourth()
         lat_wait(1, ps)
 
         @pl.loop(0, levs)
@@ -343,34 +360,30 @@
         for l in range(levs):
             ig_ref[:, l, :] = ag[l]
 
-        rc.third()
+        rd.third()
+        ra.fifth()
+        rc.fourth()
         own_cols = pl.ds(pl.multiple_of(e * wide, 128), wide)
-
-        @pl.loop(0, levs)
-        def _(l):
-            order_join((1 - e) * levs + l)
-
         fields[...] = jnp.zeros(fields.shape, F32)
 
         @pl.loop(0, levs)
         def _(l):
             fields[...] += dot(act[l], jw_ref[e * levs + l, :, own_cols], 1, 0)
 
-        ra.fourth()
         rb.third()
+        rc.fifth()
 
         @pl.loop(0, levs)
         def _(l):
             fields[...] += dot(act_in[l], jw_ref[(1 - e) * levs + l, :, own_cols], 1, 0)
+
+        rd.fourth()
 
         for m in range(levs):
             jf_ref[:, m, :] = fields[:, m * chans : (m + 1) * chans]
 
-        rc.fourth()
-        ra.fifth()
         rb.fourth()
-        rc.fifth()
-        rb.fifth()
+        rd.fifth()
 
         def put_join(half):
             def put(i, value):
@@ -379,12 +392,17 @@
 
             return put
 
-        def put_conv(i, value):
-            for tap in range(9):
-                gc_ref[i, tap // 3, tap % 3] = value[:, tap * chans : (tap + 1) * chans]
+        def put_taps(taps):
+            def put(i, value):
+                for n, tap in enumerate(taps):
+                    gc_ref[i, tap // 3, tap % 3] = value[:, n * chans : (n + 1) * chans]
+
+            return put
 
         ra.finish(put_join(e))
-        rc.finish(put_conv)
+        rc.finish(put_taps(range(FIRST_TAPS)))
+        rb.fifth()
+        rd.finish(put_taps(range(FIRST_TAPS, 9)))
         rb.finish(put_join(1 - e))
 
     def round_scratch(width):
@@ -412,16 +430,18 @@
         pltpu.VMEM((levs, cells, chans), F32),
         *round_scratch(wide),
         *round_scratch(wide),
-        *round_scratch(9 * chans),
+        *round_scratch(FIRST_TAPS * chans),
+        *round_scratch((9 - FIRST_TAPS) * chans),
         pltpu.VMEM((2 * levs, chans, 2 * wide), BF16),
         pltpu.VMEM((2 * levs, 2 * wide, chans), BF16),
         pltpu.VMEM((pl.cdiv(chans, 128), 2 * wide, 128), F32),
         pltpu.VMEM((cells, wide), F32),
+        pltpu.VMEM((levs, cells, chans), F32),
         dma((2 * levs,)),
         dma((2,)), dma((2,)), dma((4,)), dma((4,)), dma((4,)), dma((4,)),
-        dma((3,)), dma((3,)), dma((3,)), dma((3,)),
-        dma((3 * (n_lon - 1),)), dma((3 * (n_lon - 1),)),
-        dma((3,)), dma((3,)), dma((6,)), dma((6,)),
+        dma((4,)), dma((4,)), dma((4,)), dma((4,)),
+        dma((4 * (n_lon - 1),)), dma((4 * (n_lon - 1),)),
+        dma((4,)), dma((4,)), dma((8,)), dma((8,)),
     ]
     vmem = pl.BlockSpec(memory_space=pltpu.VMEM)
     return pl.pallas_call(

time: 96.1 us -> 85 us (0.88)
  the two profiles are of different devices: /device:TPU:9 before, /device:TPU:0 now
where the time goes in v3:
time: 85 us; the launch traced here: 84.7 us
  Pallas kernels  73.2 us (86%)
  local copies, waits for them, and re-layouts  10.9 us (13%)
    pallas_call x1, Pallas kernels, per_device(): run(jnp.transpose(features, (2, 0, 1, 3)), conv_weight, join_weight.resha...  73.2 us
    unnamed x11, local copies, waits for them, and re-layouts  8.62 us
    reshape x1, local copies, waits for them, and re-layouts, per_device(): joined_grad.reshape(rows * cols, levs * chans)  2.25 us

profile of v3, /device:TPU:0, one launch (start us, length us, event | category | flops | bytes accessed | tf_op | source)
XLA Modules:
  0.0 84.7 jit_solution(325321519361930359)
XLA Ops:
  0.6 2.3 %reshape.24.jg_ref = bf16[256,768]{1,0:T(8,128)(2,1)} reshape(bf16[8,32,4,192]{3,2,1,0:T(4,128)(2,1)} %param.7) | data formatting | bytes 786432 | tf_op jit(solution)/shard_map/reshape | solution.py:475
  2.9 1.9 %copy.10 = bf16[8,32,4,192]{3,1,0,2:T(8,128)(2,1)} copy(bf16[8,32,4,192]{3,2,1,0:T(4,128)(2,1)} %param.4) | data formatting | bytes 786432 | tf_op args[0]
  4.8 73.2 %shard_map.75 = (f32[256,4,192]{2,1,0:T(4,128)}, f32[256,4,192]{2,1,0:T(4,128)}, f32[2,4,48,4,192]{4,3,2,1,0:T(4,128)}, f32[4,3,3,48,192]{4,3,2,1,0:T(8,128)}) custom-call(bf16[4,8,32,192]{3,2,1,0:T(8,128)(2,1)} %bitcast.8, bf16[4,3,3,192,192]{4,3,2,1,0:T(8,128)(2,1)} %cw_ref.1, bf16[8,1536,192]{2,1,0:T(8,128)(2,1)} %bitcast.7, bf16[256,768]{1,0:T(8,128)(2,1)} %reshape.24.jg_ref), custom_call_target="tpu_custom_call" | custom-call | tf_op jit(solution)/shard_map/pallas_call | solution.py:471
  78.0 0.0 copy-start.2
  78.0 0.0 copy-start
  78.1 2.5 %copy.15 = f32[8,32,4,192]{3,2,1,0:T(4,128)} copy(f32[8,32,4,192]{3,2,1,0:T(4,128)} %bitcast.11) | data formatting | bytes 1572864
  80.6 0.0 copy-done.2
  80.6 1.0 %copy.16 = f32[8,32,4,192]{3,2,1,0:T(4,128)} copy(f32[8,32,4,192]{3,2,1,0:T(4,128)S(1)} %bitcast.10) | data formatting | bytes 1572864
  81.6 0.0 copy-done
  81.6 0.0 copy-start.1
  81.6 1.2 %copy.17 = f32[4,3,3,48,192]{4,3,2,1,0:T(8,128)} copy(f32[4,3,3,48,192]{4,3,2,1,0:T(8,128)S(1)} %copy-done) | data formatting | bytes 2654208
  82.8 0.8 copy-done.1
  83.6 1.1 %copy.18 = f32[8,48,4,192]{3,2,1,0:T(4,128)} copy(f32[8,48,4,192]{3,2,1,0:T(4,128)S(1)} %bitcast.9) | data formatting | bytes 2359296
Async XLA Ops:
  78.0 2.5 %copy-start.2 = (f32[256,4,192]{2,1,0:T(4,128)S(1)}, f32[256,4,192]{2,1,0:T(4,128)}, u32[]{:S(2)}) copy-start(f32[256,4,192]{2,1,0:T(4,128)} %get-tuple-element.9) | copy-start | bytes 2359300
  78.0 3.5 %copy-start = (f32[4,3,3,48,192]{4,3,2,1,0:T(8,128)S(1)}, f32[4,3,3,48,192]{4,3,2,1,0:T(8,128)}, u32[]{:S(2)}) copy-start(f32[4,3,3,48,192]{4,3,2,1,0:T(8,128)} %get-tuple-element.18) | copy-start | bytes 3981316
  81.6 2.0 %copy-start.1 = (f32[2,4,48,4,192]{4,3,2,1,0:T(4,128)S(1)}, f32[2,4,48,4,192]{4,3,2,1,0:T(4,128)}, u32[]{:S(2)}) copy-start(f32[2,4,48,4,192]{4,3,2,1,0:T(4,128)} %get-tuple-element.11) | copy-start | bytes 3538948

commit v4 on v3

--- a/solution.py
+++ b/solution.py
@@ -24,9 +24,9 @@
     wide = levs * chans
 
     def kernel(
-        x_ref, cw_ref, raw_ref, jg_ref,
+        x_ref, cw_ref, raw_ref, grad_ref,
         jf_ref, ig_ref, gj_ref, gc_ref,
-        jg_in, edge_out, edge_in, xs, ps, act, act_in, ag,
+        jg_ref, by_cell, jg_in, edge_out, edge_in, xs, ps, act, act_in, ag,
         own_a, s1_a, r1_a, s2_a, r2_a, s3_a, r3_a, g_a,
         own_b, s1_b, r1_b, s2_b, r2_b, s3_b, r3_b, g_b,
         own_c, s1_c, r1_c, s2_c, r2_c, s3_c, r3_c, g_c,
@@ -87,9 +87,6 @@
                 device_id=where, device_id_type=MESH,
             )
 
-        jg_copy = remote(jg_ref, jg_in, lev_send.at[0], lev_recv.at[0], {"lev": 1 - e})
-        jg_copy.start()
-
         def edge_copies(n):
             return (
                 remote(
@@ -159,13 +156,20 @@
                 lat_up(n, dst).wait_send()
                 lat_down(n, dst).wait_recv()
 
-        @pl.loop(0, levs)
-        def _(l):
-            put_middle(0, xs, l, x_ref[l].astype(F32))
+        by_cell[...] = x_ref[...].astype(F32)
+        for l in range(levs):
+            put_middle(0, xs, l, by_cell[:, l, :].reshape(rows, cols, chans))
 
         edges = edge_copies(0)
         for c in edges:
             c.start()
+
+        by_cell[...] = grad_ref[...].astype(F32)
+        for l in range(levs):
+            jg_ref[:, l * chans : (l + 1) * chans] = by_cell[:, l, :].astype(BF16)
+
+        jg_copy = remote(jg_ref, jg_in, lev_send.at[0], lev_recv.at[0], {"lev": 1 - e})
+        jg_copy.start()
 
         @pl.loop(0, levs)
         def _(l):
@@ -420,6 +424,8 @@
 
     dma = pltpu.SemaphoreType.DMA
     scratch = [
+        pltpu.VMEM((cells, wide), BF16),
+        pltpu.VMEM((cells, levs, chans), F32),
         pltpu.VMEM((cells, wide), BF16),
         pltpu.VMEM((4, levs, rows, chans), F32),
         pltpu.VMEM((4, levs, rows, chans), F32),
@@ -469,10 +475,10 @@
     scale = 1.0 / math.sqrt(rows * n_lat * cols * n_lon)
     run = make_kernel(n_lon, n_lat, rows, cols, levs, chans, scale)
     jf, ig, gj, gc = run(
-        jnp.transpose(features, (2, 0, 1, 3)),
+        features.reshape(rows * cols, levs, chans),
         conv_weight,
         join_weight.reshape(lev_total, chans * lev_total, chans),
-        joined_grad.reshape(rows * cols, levs * chans),
+        joined_grad.reshape(rows * cols, levs, chans),
     )
     return (
         jf.reshape(features.shape),

time: 85 us -> 82.2 us (0.967)
  local copies, waits for them, and re-layouts: 10.9 us -> 6.69 us
  Pallas kernels: 73.2 us -> 74.7 us
    reshape x1 -> x0, local copies, waits for them, and re-layouts: 2.25 us -> none  [per_device(): joined_grad.reshape(rows * cols, levs * chans)]
    unnamed x11 -> x10, local copies, waits for them, and re-layouts: 8.62 us -> 6.69 us
    pallas_call x1, Pallas kernels: 73.2 us -> 74.7 us  [per_device(): run(features.reshape(rows * cols, levs, chans), conv_weight, join_weight....]
where the time goes in v4:
time: 82.2 us; the launch traced here: 82 us
  Pallas kernels  74.7 us (91%)
  local copies, waits for them, and re-layouts  6.69 us (8%)
    pallas_call x1, Pallas kernels, per_device(): run(features.reshape(rows * cols, levs, chans), conv_weight, join_weight....  74.7 us
    unnamed x10, local copies, waits for them, and re-layouts  6.69 us

profile of v4, /device:TPU:0, one launch (start us, length us, event | category | flops | bytes accessed | tf_op | source)
XLA Modules:
  0.0 82.0 jit_solution(27588393811131952)
XLA Ops:
  0.6 74.7 %shard_map.75 = (f32[256,4,192]{2,1,0:T(4,128)}, f32[256,4,192]{2,1,0:T(4,128)}, f32[2,4,48,4,192]{4,3,2,1,0:T(4,128)}, f32[4,3,3,48,192]{4,3,2,1,0:T(8,128)}) custom-call(bf16[256,4,192]{2,1,0:T(4,128)(2,1)} %bitcast.10, bf16[4,3,3,192,192]{4,3,2,1,0:T(8,128)(2,1)} %cw_ref.1, bf16[8,1536,192]{2,1,0:T(8,128)(2,1)} %bitcast.6, bf16[256,4,192]{2,1,0:T(4,128)(2,1)} %bitcast.11), custom_call_target="tpu_custom_call" | custom-call | tf_op jit(solution)/shard_map/pallas_call | solution.py:477
  75.3 0.0 copy-start.2
  75.3 0.0 copy-start
  75.3 2.5 %copy.12 = f32[8,32,4,192]{3,2,1,0:T(4,128)} copy(f32[8,32,4,192]{3,2,1,0:T(4,128)} %bitcast.9) | data formatting | bytes 1572864
  77.8 0.0 copy-done.2
  77.8 1.0 %copy.13 = f32[8,32,4,192]{3,2,1,0:T(4,128)} copy(f32[8,32,4,192]{3,2,1,0:T(4,128)S(1)} %bitcast.8) | data formatting | bytes 1572864
  78.8 0.0 copy-done
  78.8 0.0 copy-start.1
  78.8 1.2 %copy.14 = f32[4,3,3,48,192]{4,3,2,1,0:T(8,128)} copy(f32[4,3,3,48,192]{4,3,2,1,0:T(8,128)S(1)} %copy-done) | data formatting | bytes 2654208
  80.0 0.8 %copy-done.1 = f32[2,4,48,4,192]{4,3,2,1,0:T(4,128)S(1)} copy-done((f32[2,4,48,4,192]{4,3,2,1,0:T(4,128)S(1)}, f32[2,4,48,4,192]{4,3,2,1,0:T(4,128)}, u32[]{:S(2)}) %copy-start.1) | copy-done | bytes 1179672
  80.9 1.1 %copy.15 = f32[8,48,4,192]{3,2,1,0:T(4,128)} copy(f32[8,48,4,192]{3,2,1,0:T(4,128)S(1)} %bitcast.7) | data formatting | bytes 2359296
Async XLA Ops:
  75.3 2.5 %copy-start.2 = (f32[256,4,192]{2,1,0:T(4,128)S(1)}, f32[256,4,192]{2,1,0:T(4,128)}, u32[]{:S(2)}) copy-start(f32[256,4,192]{2,1,0:T(4,128)} %get-tuple-element.9) | copy-start | bytes 2359300
  75.3 3.5 %copy-start = (f32[4,3,3,48,192]{4,3,2,1,0:T(8,128)S(1)}, f32[4,3,3,48,192]{4,3,2,1,0:T(8,128)}, u32[]{:S(2)}) copy-start(f32[4,3,3,48,192]{4,3,2,1,0:T(8,128)} %get-tuple-element.18) | copy-start | bytes 3981316
  78.8 2.0 %copy-start.1 = (f32[2,4,48,4,192]{4,3,2,1,0:T(4,128)S(1)}, f32[2,4,48,4,192]{4,3,2,1,0:T(4,128)}, u32[]{:S(2)}) copy-start(f32[2,4,48,4,192]{4,3,2,1,0:T(4,128)} %get-tuple-element.11) | copy-start | bytes 3538948

commit v5 on v4

--- a/solution.py
+++ b/solution.py
@@ -339,14 +339,14 @@
         rd.first(fill_taps(range(FIRST_TAPS, 9)))
         ra.third()
         rd.second()
+        @pl.loop(0, levs)
+        def _(l):
+            order_join((1 - e) * levs + l)
+
         act_copy.wait()
         rb.first(fill_other)
         rc.third()
         rb.second()
-
-        @pl.loop(0, levs)
-        def _(l):
-            order_join((1 - e) * levs + l)
 
         ra.fourth()
         lat_wait(1, ps)

time: 82.2 us -> 82.2 us (level)
  no operation moved by 1% of the time
where the time goes in v5:
time: 82.2 us; the launch traced here: 82 us
  Pallas kernels  74.7 us (91%)
  local copies, waits for them, and re-layouts  6.69 us (8%)
    pallas_call x1, Pallas kernels, per_device(): run(features.reshape(rows * cols, levs, chans), conv_weight, join_weight....  74.7 us
    unnamed x10, local copies, waits for them, and re-layouts  6.69 us

profile of v5, /device:TPU:0, one launch (start us, length us, event | category | flops | bytes accessed | tf_op | source)
XLA Modules:
  0.0 82.0 jit_solution(1973342321040254446)
XLA Ops:
  0.6 74.7 %shard_map.75 = (f32[256,4,192]{2,1,0:T(4,128)}, f32[256,4,192]{2,1,0:T(4,128)}, f32[2,4,48,4,192]{4,3,2,1,0:T(4,128)}, f32[4,3,3,48,192]{4,3,2,1,0:T(8,128)}) custom-call(bf16[256,4,192]{2,1,0:T(4,128)(2,1)} %bitcast.10, bf16[4,3,3,192,192]{4,3,2,1,0:T(8,128)(2,1)} %cw_ref.1, bf16[8,1536,192]{2,1,0:T(8,128)(2,1)} %bitcast.6, bf16[256,4,192]{2,1,0:T(4,128)(2,1)} %bitcast.11), custom_call_target="tpu_custom_call" | custom-call | tf_op jit(solution)/shard_map/pallas_call | solution.py:477
  75.3 0.0 copy-start.2
  75.3 0.0 copy-start
  75.3 2.5 %copy.12 = f32[8,32,4,192]{3,2,1,0:T(4,128)} copy(f32[8,32,4,192]{3,2,1,0:T(4,128)} %bitcast.9) | data formatting | bytes 1572864
  77.8 0.0 copy-done.2
  77.9 1.0 %copy.13 = f32[8,32,4,192]{3,2,1,0:T(4,128)} copy(f32[8,32,4,192]{3,2,1,0:T(4,128)S(1)} %bitcast.8) | data formatting | bytes 1572864
  78.8 0.0 copy-done
  78.8 0.0 copy-start.1
  78.8 1.2 %copy.14 = f32[4,3,3,48,192]{4,3,2,1,0:T(8,128)} copy(f32[4,3,3,48,192]{4,3,2,1,0:T(8,128)S(1)} %copy-done) | data formatting | bytes 2654208
  80.0 0.8 %copy-done.1 = f32[2,4,48,4,192]{4,3,2,1,0:T(4,128)S(1)} copy-done((f32[2,4,48,4,192]{4,3,2,1,0:T(4,128)S(1)}, f32[2,4,48,4,192]{4,3,2,1,0:T(4,128)}, u32[]{:S(2)}) %copy-start.1) | copy-done | bytes 1179672
  80.9 1.1 %copy.15 = f32[8,48,4,192]{3,2,1,0:T(4,128)} copy(f32[8,48,4,192]{3,2,1,0:T(4,128)S(1)} %bitcast.7) | data formatting | bytes 2359296
Async XLA Ops:
  75.3 2.5 %copy-start.2 = (f32[256,4,192]{2,1,0:T(4,128)S(1)}, f32[256,4,192]{2,1,0:T(4,128)}, u32[]{:S(2)}) copy-start(f32[256,4,192]{2,1,0:T(4,128)} %get-tuple-element.9) | copy-start | bytes 2359300
  75.3 3.5 %copy-start = (f32[4,3,3,48,192]{4,3,2,1,0:T(8,128)S(1)}, f32[4,3,3,48,192]{4,3,2,1,0:T(8,128)}, u32[]{:S(2)}) copy-start(f32[4,3,3,48,192]{4,3,2,1,0:T(8,128)} %get-tuple-element.18) | copy-start | bytes 3981316
  78.8 2.0 %copy-start.1 = (f32[2,4,48,4,192]{4,3,2,1,0:T(4,128)S(1)}, f32[2,4,48,4,192]{4,3,2,1,0:T(4,128)}, u32[]{:S(2)}) copy-start(f32[2,4,48,4,192]{4,3,2,1,0:T(4,128)} %get-tuple-element.11) | copy-start | bytes 3538948
